TPU v7x, 32 devices: a whole 2x2x4 slice. The times are simulated.
32 devices in a mesh: row: 2 (over y), col: 4 (over z), depth: 4 (over x, core).
Axes of the slice: x: 2, y: 2, z: 4, core: 2. Of those that a mesh axis runs over, the one named last changes fastest.
Arguments:
- integrals: float32 [4096, 4096], P(('row', 'col'), 'depth'), may hold values from -0.09375 to 0.09375
- amplitudes: float32 [4096, 64, 64], P('depth', 'col', 'row'), may hold values from -6 to 6
Outputs:
- relaid: float32 [64, 64, 4096], P(('col', 'depth'), 'row')
All inputs are finite; a program needn't handle non-finite values.
Results may differ from a plain program's by a relative error of at most 0.00007.
Values sent between devices are 32-bit elements; how exact they have to be, the bound alone decides.
A program may use at most 64 MiB of HBM per device.

v0:
```python
import jax
import jax.numpy as jnp
from jax import lax
from jax.sharding import PartitionSpec as P


def shards(integrals, amplitudes):
    rows_w = lax.all_gather(integrals, "col", axis=0, tiled=True)
    panel_t = lax.all_gather(amplitudes, "row", axis=2, tiled=True)
    kc_rows, i_count, j_count = panel_t.shape
    flat_panel = panel_t.reshape(kc_rows, i_count * j_count)
    row_count = lax.axis_size("row")
    ab_rows = rows_w.shape[0]
    summed = lax.psum_scatter(
        lax.dot_general(
            flat_panel,
            rows_w,
            (((0,), (1,)), ((), ())),
            precision=lax.Precision.HIGHEST,
            preferred_element_type=jnp.float32,
        ),
        "depth",
        scatter_dimension=0,
        tiled=True,
    )
    shares = summed.reshape(-1, j_count // row_count, row_count, ab_rows)
    exchanged = lax.all_to_all(shares, "row", split_axis=2, concat_axis=3, tiled=True)
    result = exchanged.reshape(shares.shape[0], j_count // row_count, row_count * ab_rows)
    return result


def solution(mesh):
    placed = (P(("row", "col"), "depth"), P("depth", "col", "row"))
    return jax.shard_map(
        shards,
        mesh=mesh,
        in_specs=placed,
        out_specs=P(("col", "depth"), "row", None),
        check_vma=False,
    )
```

profile of v0, /device:TPU:0, one launch (start us, length us, event | category | flops | bytes accessed | tf_op | source)
XLA Modules:
  0.0 360.1 jit_solution(9074562860716130166)
XLA Ops:
  6.5 0.0 all-gather.3.cloned.1.call-start
  6.5 0.7 all-gather.3.cloned.1.call-update
  7.3 0.0 all-gather.5.cloned.1.call-start
  7.3 0.7 all-gather.5.cloned.1.call-update
  8.0 0.0 reduce-scatter.2.cloned.1.call-start
  8.1 60.3 %all-gather.3.cloned.1.call-done = f32[1024,16,64]{0,2,1:T(8,128)} async-done(((f32[1024,16,32]{0,2,1:T(8,128)}), f32[1024,16,64]{0,2,1:T(8,128)}) %all-gather.3.cloned.1.call-update) | async-done | bytes 4194320 | tf_op jit(solution)/shard_map/all_gather | solution.py:9
  68.4 151.2 %all-gather.5.cloned.1.call-done = f32[2048,1024]{1,0:T(8,128)} async-done(((f32[512,1024]{1,0:T(8,128)}), f32[2048,1024]{1,0:T(8,128)}) %all-gather.5.cloned.1.call-update) | async-done | bytes 8388624 | tf_op jit(solution)/shard_map/all_gather | solution.py:8
  219.6 31.0 %fusion = f32[1024,2048]{1,0:T(8,128)} fusion(f32[1024,1024]{0,1:T(8,128)} %bitcast.6, f32[2048,1024]{1,0:T(8,128)} %all-gather.5.cloned.1.call-done), kind=kOutput, calls=%fused_computation | convolution fusion | flops 25769803776 | bytes 20971520 | tf_op jit(solution)/shard_map/dot_general | solution.py:15
  250.7 0.0 reduce-scatter.2.cloned.1.call-update
  250.7 70.1 %reduce-scatter.2.cloned.1.call-done = f32[256,2048]{1,0:T(8,128)} async-done(((f32[1024,2048]{1,0:T(8,128)}), f32[256,2048]{1,0:T(8,128)}) %reduce-scatter.2.cloned.1.call-update) | async-done | bytes 2097168 | tf_op jit(solution)/shard_map/reduce_scatter | solution.py:14
  320.8 2.5 reshape.14
  323.3 1.2 copy.4
  324.5 27.7 %all_to_all.4 = f32[4,32,2,2048]{3,1,0,2:T(8,128)S(1)} all-to-all(f32[4,32,2,2048]{3,1,0,2:T(8,128)S(1)} %copy.4), channel_id=1, replica_groups=mesh['row'=2,'col'=4,'depth'=4] {'row'}, dimensions={2} | all-to-all | bytes 4194304 | tf_op jit(solution)/shard_map/all_to_all | solution.py:27
  352.1 1.5 copy.6
Async XLA Ops:
  6.5 61.8 %all-gather.3.cloned.1.call-start = ((), (), s32[]{:S(2)}) async-start(), calls=%async_computation.2 | async-start | bytes 6291456 | tf_op jit(solution)/shard_map/all_gather | solution.py:9
  7.3 212.4 %all-gather.5.cloned.1.call-start = ((), (), s32[]{:S(2)}) async-start(), calls=%async_computation.3 | async-start | bytes 10485760 | tf_op jit(solution)/shard_map/all_gather | solution.py:8
  8.0 312.8 %reduce-scatter.2.cloned.1.call-start = ((), (), s32[]{:S(2)}) async-start(), calls=%async_computation.4 | async-start | bytes 10485760 | tf_op jit(solution)/shard_map/reduce_scatter | solution.py:14
Sparse Core Ops, SparseCore 0:
  8.9 59.4 all-gather.2
  69.9 149.6 all-gather.4
  250.8 69.9 reduce-scatter.1
where the time goes:
time: 360 us
  waiting for transfers between devices  283 us (79%)
  matrix products  31 us (9%)
  blocking collectives  27.7 us (8%)
  between operations  13.1 us (4%)
  local copies, waits for them, and re-layouts  5.17 us (1%)
    all_gather x1, waiting for transfers between devices, shards(): rows_w = lax.all_gather(integrals, 'col', axis=0, tiled=True)  151 us
    reduce_scatter x1, waiting for transfers between devices, shards(): lax.psum_scatter(lax.dot_general(flat_panel, rows_w, (((0,), (1,)), ((),...  70.1 us
    all_gather x1, waiting for transfers between devices, shards(): panel_t = lax.all_gather(amplitudes, 'row', axis=2, tiled=True)  60.3 us
    dot_general x1, matrix products, shards(): lax.dot_general(flat_panel, rows_w, (((0,), (1,)), ((), ())), precision=l...  31 us
    all_to_all x1, blocking collectives, shards(): lax.all_to_all(shares, 'row', split_axis=2, concat_axis=3, tiled=True)  27.7 us
  transfers between devices with their start and end apart: 3, of which 3 were waited for; matrix products, arithmetic and copies ran while one was open for 0% of the time, Pallas kernels for 0%

commit v1 on v0

v1 whole, which is shorter than its diff:
```python
import functools

import jax
import jax.numpy as jnp
import numpy as np
from jax import lax
from jax.experimental import pallas as pl
from jax.experimental.pallas import tpu as pltpu
from jax.sharding import PartitionSpec as P

MESH = pl.DeviceIdType.MESH
CHUNK = 256
LANES = 2


def halves(x):
    hi = x.astype(jnp.bfloat16)
    lo = (x - hi.astype(jnp.float32)).astype(jnp.bfloat16)
    return hi, lo


def kernel(sizes, gathered, w_ref, t_ref, order_ref, out_ref, wg, tg, th, tl, part, recv1, recv2, fin,
           own_sem, w_send, w_recv, t_send, t_recv, s1_send, s1_recv, s2_send, s2_recv, r_send, r_recv):
    n_row, n_col, n_depth = sizes
    n_lo = LANES
    n_hi = n_depth // n_lo
    ab_rows = w_ref.shape[0]
    n_ch = ab_rows // CHUNK
    steps = n_col * n_ch
    rows_all = th.shape[0]
    rows_lo = rows_all // n_lo
    rows_d = rows_lo // n_hi
    rows_r = rows_d // n_row
    row, col, depth = lax.axis_index("row"), lax.axis_index("col"), lax.axis_index("depth")
    hi, lo = depth // n_lo, depth % n_lo

    def row_peer(o):
        return (row + o) % n_row

    def hi_peer(o):
        return (hi + o) % n_hi

    mate = hi * n_lo + (1 - lo)

    barrier = pltpu.get_barrier_semaphore()
    for o in range(1, n_row):
        pl.semaphore_signal(barrier, inc=1, device_id={"row": row_peer(o)}, device_id_type=MESH)
    pl.semaphore_signal(barrier, inc=1, device_id={"depth": mate}, device_id_type=MESH)
    for o in range(1, n_hi):
        pl.semaphore_signal(barrier, inc=1, device_id={"depth": hi_peer(o) * n_lo + lo}, device_id_type=MESH)

    @pl.when(col > 0)
    def _():
        pl.semaphore_signal(barrier, inc=1, device_id={"col": col - 1}, device_id_type=MESH)

    @pl.when(col < n_col - 1)
    def _():
        pl.semaphore_signal(barrier, inc=1, device_id={"col": col + 1}, device_id_type=MESH)

    fixed = (n_row - 1) + 1 + (n_hi - 1)
    ends = jnp.where(col > 0, 1, 0) + jnp.where(col < n_col - 1, 1, 0)
    pl.semaphore_wait(barrier, fixed + ends)

    def w_copy(src, b, h, side):
        rows = pl.ds(pl.multiple_of(h * CHUNK, CHUNK), CHUNK)
        to = jnp.clip(col + (1 if side else -1), 0, n_col - 1)
        return pltpu.make_async_remote_copy(
            src_ref=w_ref.at[rows] if src is None else wg.at[b, rows],
            dst_ref=wg.at[b, rows],
            send_sem=w_send.at[side, b, h],
            recv_sem=w_recv.at[b, h],
            device_id={"col": to},
            device_id_type=MESH,
        )

    def send_own(h, c):
        @pl.when(col > 0)
        def _():
            w_copy(None, col, h, 0).start()

        @pl.when(col < n_col - 1)
        def _():
            w_copy(None, col, h, 1).start()

        return c

    lax.fori_loop(0, n_ch, send_own, 0)

    def t_copy(o):
        return pltpu.make_async_remote_copy(
            src_ref=t_ref,
            dst_ref=tg.at[row],
            send_sem=t_send.at[o - 1],
            recv_sem=t_recv.at[o - 1],
            device_id={"row": row_peer(o)},
            device_id_type=MESH,
        )

    if not gathered:
        for o in range(1, n_row):
            t_copy(o).start()
        t_own = pltpu.make_async_copy(t_ref, tg.at[row], own_sem.at[1])
    else:
        t_own = pltpu.make_async_copy(t_ref, tg, own_sem.at[1])
    t_own.start()
    w_own = pltpu.make_async_copy(w_ref, wg.at[col], own_sem.at[0])
    w_own.start()

    def place(q):
        i_count, j_local, kc = t_ref.shape
        i_out = i_count // n_depth
        per_r = j_local // n_row
        order = order_ref[...]

        def body(d, c):
            x = tg[q, pl.ds(d * i_out, i_out)].reshape(i_out * j_local, kc)
            base = (d % n_lo) * rows_lo + (d // n_lo) * rows_d
            for x_part, into in zip(halves(x), (th, tl)):
                y = jnp.dot(order, x_part, preferred_element_type=jnp.float32).astype(jnp.bfloat16)
                for piece in range(n_row * i_out):
                    at = base + piece * (per_r * n_row) + q * per_r
                    into[pl.ds(pl.multiple_of(at, per_r), per_r), :] = y[piece * per_r : (piece + 1) * per_r]
            return c

        lax.fori_loop(0, n_depth, body, 0)

    t_own.wait()
    if not gathered:
        place(row)
    else:
        def body(m, c):
            at = pl.ds(pl.multiple_of(m * 64, 64), 64)
            th[at, :], tl[at, :] = halves(tg[at, :])
            return c

        lax.fori_loop(0, rows_all // 64, body, 0)

    def forward(b, h):
        w_copy(wg, b, h, 0).wait_recv()

        @pl.when((b < col) & (col < n_col - 1))
        def _():
            w_copy(wg, b, h, 1).start()

        @pl.when((b > col) & (col > 0))
        def _():
            w_copy(wg, b, h, 0).start()

    def first(h, c):
        @pl.when(col > 0)
        def _():
            forward(col - 1, h)

        @pl.when(col < n_col - 1)
        def _():
            forward(col + 1, h)

        return c

    lax.fori_loop(0, n_ch, first, 0)

    if not gathered:
        for o in range(1, n_row):
            t_copy(o).wait_recv()
            place((row + n_row - o) % n_row)
    w_own.wait()

    near = jnp.minimum(col, n_col - 1 - col)

    def block_at(k):
        p, h = k // n_ch, k % n_ch
        both = p <= 2 * near
        s = jnp.where(both, (p + 1) // 2, p - near)
        left = jnp.where(both, p % 2 == 1, col > near)
        b = jnp.where(p == 0, col, jnp.where(left, col - s, col + s))
        return b, h, s

    def s1_copy(k):
        return pltpu.make_async_remote_copy(
            src_ref=part.at[k, pl.ds(pl.multiple_of((1 - lo) * rows_lo, rows_lo), rows_lo)],
            dst_ref=recv1.at[k],
            send_sem=s1_send.at[k],
            recv_sem=s1_recv.at[k],
            device_id={"depth": mate},
            device_id_type=MESH,
        )

    def s2_copy(k, o):
        return pltpu.make_async_remote_copy(
            src_ref=part.at[k, pl.ds(pl.multiple_of(lo * rows_lo + hi_peer(o) * rows_d, rows_d), rows_d)],
            dst_ref=recv2.at[k, o - 1],
            send_sem=s2_send.at[k, o - 1],
            recv_sem=s2_recv.at[k, o - 1],
            device_id={"depth": hi_peer(o) * n_lo + lo},
            device_id_type=MESH,
        )

    def out_cols(k):
        b, h, _ = block_at(k)
        return pl.ds(pl.multiple_of((row * n_col + b) * ab_rows + h * CHUNK, CHUNK), CHUNK)

    def r_copy(k, o):
        return pltpu.make_async_remote_copy(
            src_ref=fin.at[k, pl.ds(pl.multiple_of(row_peer(o) * rows_r, rows_r), rows_r)],
            dst_ref=out_ref.at[:, out_cols(k)],
            send_sem=r_send.at[k, o - 1],
            recv_sem=r_recv.at[k, o - 1],
            device_id={"row": row_peer(o)},
            device_id_type=MESH,
        )

    def dot(a, b):
        return lax.dot_general(a, b, (((1,), (1,)), ((), ())), preferred_element_type=jnp.float32)

    def step(k, c):
        @pl.when(k < steps)
        def _():
            b, h, s = block_at(k)

            @pl.when(s >= 2)
            def _():
                forward(b, h)

            wh, wl = halves(wg[b, pl.ds(pl.multiple_of(h * CHUNK, CHUNK), CHUNK), :])
            tile = rows_all // 2
            for m in range(2):
                at = pl.ds(m * tile, tile)
                a = th[at, :]
                part[k, at, :] = dot(a, wh) + dot(a, wl) + dot(tl[at, :], wh)
            s1_copy(k).start()

        @pl.when((k >= 1) & (k < steps + 1))
        def _():
            j = k - 1
            s1_copy(j).wait_recv()
            at = pl.ds(pl.multiple_of(lo * rows_lo, rows_lo), rows_lo)
            part[j, at, :] = part[j, at, :] + recv1[j]
            for o in range(1, n_hi):
                s2_copy(j, o).start()

        @pl.when(k >= 2)
        def _():
            j = k - 2
            total = part[j, pl.ds(pl.multiple_of(lo * rows_lo + hi * rows_d, rows_d), rows_d), :]
            for o in range(1, n_hi):
                s2_copy(j, o).wait_recv()
                total = total + recv2[j, o - 1]
            fin[j] = total
            for o in range(1, n_row):
                r_copy(j, o).start()
            out_ref[:, out_cols(j)] = fin[j, pl.ds(pl.multiple_of(row * rows_r, rows_r), rows_r), :]

        return c

    lax.fori_loop(0, steps + 2, step, 0)

    def drain(k, c):
        s1_copy(k).wait_send()
        for o in range(1, n_hi):
            s2_copy(k, o).wait_send()
        for o in range(1, n_row):
            r_copy(k, o).wait_send()
            r_copy(k, o).wait_recv()
        b, h = k // n_ch, k % n_ch

        @pl.when((b <= col) & (col < n_col - 1))
        def _():
            w_copy(wg, b, h, 1).wait_send()

        @pl.when((b >= col) & (col > 0))
        def _():
            w_copy(wg, b, h, 0).wait_send()

        return c

    lax.fori_loop(0, steps, drain, 0)
    if not gathered:
        for o in range(1, n_row):
            t_copy(o).wait_send()


def shards(sizes, integrals, amplitudes):
    n_row, n_col, n_depth = sizes
    n_lo = LANES
    n_hi = n_depth // n_lo
    kc, i_count, j_local = amplitudes.shape
    j_count = j_local * n_row
    ab_rows = integrals.shape[0]
    steps = n_col * (ab_rows // CHUNK)
    rows_all = i_count * j_count
    rows_lo = rows_all // n_lo
    rows_d = rows_lo // n_hi
    rows_r = rows_d // n_row
    i_out = i_count // n_depth
    gathered = j_local % (16 * n_row) != 0
    side = i_out * j_local
    tiny = j_local if gathered else n_row
    source = np.arange(side).reshape(i_out, j_local // tiny, tiny).transpose(2, 0, 1).reshape(-1)
    order = jnp.asarray(np.eye(side)[source], jnp.bfloat16)
    t = jnp.transpose(amplitudes, (1, 2, 0))
    if gathered:
        t = lax.all_gather(t, "row", axis=1, tiled=True)
        t = t.reshape(n_hi, n_lo, i_out, j_count // n_row, n_row, kc)
        t = jnp.transpose(t, (1, 0, 4, 2, 3, 5)).reshape(rows_all, kc)
        tg = pltpu.VMEM(t.shape, jnp.float32)
    else:
        tg = pltpu.VMEM((n_row,) + t.shape, jnp.float32)
    dma = pltpu.SemaphoreType.DMA
    out = pl.pallas_call(
        functools.partial(kernel, sizes, gathered),
        out_shape=jax.ShapeDtypeStruct((rows_r, n_row * n_col * ab_rows), jnp.float32),
        in_specs=[pl.BlockSpec(memory_space=pl.ANY)] * 2 + [pl.BlockSpec(memory_space=pltpu.VMEM)],
        out_specs=pl.BlockSpec(memory_space=pltpu.VMEM),
        scratch_shapes=[
            pltpu.VMEM((n_col, ab_rows, kc), jnp.float32),
            tg,
            pltpu.VMEM((rows_all, kc), jnp.bfloat16),
            pltpu.VMEM((rows_all, kc), jnp.bfloat16),
            pltpu.VMEM((steps, rows_all, CHUNK), jnp.float32),
            pltpu.VMEM((steps, rows_lo, CHUNK), jnp.float32),
            pltpu.VMEM((steps, max(n_hi - 1, 1), rows_d, CHUNK), jnp.float32),
            pltpu.VMEM((steps, rows_d, CHUNK), jnp.float32),
            dma((2,)),
            dma((2, n_col, ab_rows // CHUNK)),
            dma((n_col, ab_rows // CHUNK)),
            dma((max(n_row - 1, 1),)),
            dma((max(n_row - 1, 1),)),
            dma((steps,)),
            dma((steps,)),
            dma((steps, max(n_hi - 1, 1))),
            dma((steps, max(n_hi - 1, 1))),
            dma((steps, max(n_row - 1, 1))),
            dma((steps, max(n_row - 1, 1))),
        ],
        compiler_params=pltpu.CompilerParams(
            collective_id=0, has_side_effects=True, vmem_limit_bytes=60 * 2**20
        ),
        cost_estimate=pl.CostEstimate(
            flops=6 * rows_all * kc * ab_rows * n_col, bytes_accessed=6 * 2**20, transcendentals=0
        ),
    )(integrals, t, order)
    return out.reshape(i_out, j_count // n_row, n_row * n_col * ab_rows)


def solution(mesh):
    sizes = (mesh.shape["row"], mesh.shape["col"], mesh.shape["depth"])
    placed = (P(("row", "col"), "depth"), P("depth", "col", "row"))
    return jax.shard_map(
        functools.partial(shards, sizes),
        mesh=mesh,
        in_specs=placed,
        out_specs=P(("col", "depth"), "row", None),
        check_vma=False,
    )
```

time: 360 us -> 165 us (0.46)
  waiting for transfers between devices: 283 us -> 0 us
  Pallas kernels: 0 us -> 162 us
  matrix products: 31 us -> 0 us
  blocking collectives: 27.7 us -> 0 us
  between operations: 13.1 us -> 0.01 us
    all_gather x2 -> x0, waiting for transfers between devices: 212 us -> none  [the longest x1 151 us: shards(): rows_w = lax.all_gather(integrals, 'col', axis=0, tiled=True)]
    pallas_call x0 -> x1, Pallas kernels: none -> 162 us  [shards(): pl.pallas_call(functools.partial(kernel, sizes, gathered), out_shape=jax....]
    reduce_scatter x1 -> x0, waiting for transfers between devices: 70.1 us -> none  [shards(): lax.psum_scatter(lax.dot_general(flat_panel, rows_w, (((0,), (1,)), ((),...]
    dot_general x1 -> x0, matrix products: 31 us -> none  [shards(): lax.dot_general(flat_panel, rows_w, (((0,), (1,)), ((), ())), precision=l...]
    all_to_all x1 -> x0, blocking collectives: 27.7 us -> none  [shards(): lax.all_to_all(shares, 'row', split_axis=2, concat_axis=3, tiled=True)]
    reshape x3 -> x0, local copies, waits for them, and re-layouts: 5.17 us -> none  [the longest x2 3.71 us: shards(): shares = summed.reshape(-1, j_count // row_count, row_count, ab_rows)]
  transfers between devices with their start and end apart: 3 -> 0, of which waited for: 3 -> 0; matrix products, arithmetic and copies ran while one was open for 0% -> 0% of each run, Pallas kernels for 0% -> 0%
where the time goes in v1:
time: 165 us
  Pallas kernels  162 us (98%)
  local copies, waits for them, and re-layouts  3.11 us (2%)
    pallas_call x1, Pallas kernels, shards(): pl.pallas_call(functools.partial(kernel, sizes, gathered), out_shape=jax....  162 us

profile of v1, /device:TPU:0, one launch (start us, length us, event | category | flops | bytes accessed | tf_op | source)
XLA Modules:
  0.0 164.9 jit_solution(9578680539301036214)
XLA Ops:
  0.0 161.7 %shard_map.37 = f32[128,4096]{1,0:T(8,128)} custom-call(f32[512,1024]{1,0:T(8,128)} %w_ref.1, f32[16,32,1024]{2,1,0:T(8,128)} %bitcast.3, bf16[128,128]{1,0:T(8,128)(2,1)} %constant.2.clone.order_ref), custom_call_target="tpu_custom_call" | custom-call | flops 12884901888 | bytes 6291456 | tf_op jit(solution)/shard_map/pallas_call | solution.py:309
  161.7 3.1 %copy.5 = f32[4,32,4096]{2,1,0:T(8,128)} copy(f32[4,32,4096]{2,1,0:T(8,128)} %bitcast.2) | data formatting | bytes 4194304

commit v2 on v1

--- a/solution.py
+++ b/solution.py
@@ -19,15 +19,16 @@
     return hi, lo
 
 
-def kernel(sizes, gathered, w_ref, t_ref, order_ref, out_ref, wg, tg, th, tl, part, recv1, recv2, fin,
-           own_sem, w_send, w_recv, t_send, t_recv, s1_send, s1_recv, s2_send, s2_recv, r_send, r_recv):
+def kernel(sizes, gathered, w_ref, t_ref, order_ref, out_ref, wg, tg, tg2, th, tl, part, recv1, recv2, fin,
+           own_sem, w_send, w_recv, t_send, t_recv, s1_send, s1_recv, s2_send, s2_recv, r_send, r_recv,
+           e_send, e_recv, x_send, x_recv, d_send, d_recv):
     n_row, n_col, n_depth = sizes
     n_lo = LANES
     n_hi = n_depth // n_lo
     ab_rows = w_ref.shape[0]
     n_ch = ab_rows // CHUNK
     steps = n_col * n_ch
-    rows_all = th.shape[0]
+    rows_all = th.shape[1]
     rows_lo = rows_all // n_lo
     rows_d = rows_lo // n_hi
     rows_r = rows_d // n_row
@@ -41,6 +42,13 @@
         return (hi + o) % n_hi
 
     mate = hi * n_lo + (1 - lo)
+    at_end = (col == 0) | (col == n_col - 1)
+    helps = (col == 1) | (col == n_col - 2)
+    far = jnp.where(col < n_col // 2, n_col - 1, 0)
+    end_col = jnp.where(col < n_col // 2, 0, n_col - 1)
+    help_col = jnp.where(col < n_col // 2, 1, n_col - 2)
+    normal = jnp.where(at_end, steps - n_ch, steps)
+    total_steps = jnp.where(helps, steps + n_ch, normal)
 
     barrier = pltpu.get_barrier_semaphore()
     for o in range(1, n_row):
@@ -57,9 +65,24 @@
     def _():
         pl.semaphore_signal(barrier, inc=1, device_id={"col": col + 1}, device_id_type=MESH)
 
+    for o in range(1, n_row):
+
+        @pl.when(at_end)
+        def _():
+            pl.semaphore_signal(
+                barrier, inc=1, device_id={"row": row_peer(o), "col": help_col}, device_id_type=MESH
+            )
+
+        @pl.when(helps)
+        def _():
+            pl.semaphore_signal(
+                barrier, inc=1, device_id={"row": row_peer(o), "col": end_col}, device_id_type=MESH
+            )
+
     fixed = (n_row - 1) + 1 + (n_hi - 1)
     ends = jnp.where(col > 0, 1, 0) + jnp.where(col < n_col - 1, 1, 0)
-    pl.semaphore_wait(barrier, fixed + ends)
+    diagonal = jnp.where(at_end | helps, n_row - 1, 0)
+    pl.semaphore_wait(barrier, fixed + ends + diagonal)
 
     def w_copy(src, b, h, side):
         rows = pl.ds(pl.multiple_of(h * CHUNK, CHUNK), CHUNK)
@@ -106,43 +129,91 @@
     w_own = pltpu.make_async_copy(w_ref, wg.at[col], own_sem.at[0])
     w_own.start()
 
-    def place(q):
+    def place(src, which, q, first, last):
         i_count, j_local, kc = t_ref.shape
         i_out = i_count // n_depth
         per_r = j_local // n_row
         order = order_ref[...]
 
         def body(d, c):
-            x = tg[q, pl.ds(d * i_out, i_out)].reshape(i_out * j_local, kc)
+            x = src[q, pl.ds(d * i_out, i_out)].reshape(i_out * j_local, kc)
             base = (d % n_lo) * rows_lo + (d // n_lo) * rows_d
             for x_part, into in zip(halves(x), (th, tl)):
                 y = jnp.dot(order, x_part, preferred_element_type=jnp.float32).astype(jnp.bfloat16)
                 for piece in range(n_row * i_out):
                     at = base + piece * (per_r * n_row) + q * per_r
-                    into[pl.ds(pl.multiple_of(at, per_r), per_r), :] = y[piece * per_r : (piece + 1) * per_r]
+                    into[which, pl.ds(pl.multiple_of(at, per_r), per_r), :] = y[piece * per_r : (piece + 1) * per_r]
             return c
 
-        lax.fori_loop(0, n_depth, body, 0)
+        lax.fori_loop(first, last, body, 0)
+
+    def plain(src, which, first, last):
+        def body(m, c):
+            at = pl.ds(pl.multiple_of(m * 64, 64), 64)
+            th[which, at, :], tl[which, at, :] = halves(src[at, :])
+            return c
+
+        lax.fori_loop(first * (rows_all // 64) // n_depth, last * (rows_all // 64) // n_depth, body, 0)
+
+    piece = t_ref.shape[0] // n_depth
+
+    def e_copy(p):
+        rows = pl.ds(p * piece, piece)
+        return pltpu.make_async_remote_copy(
+            src_ref=t_ref.at[rows],
+            dst_ref=tg2.at[rows] if gathered else tg2.at[row, rows],
+            send_sem=e_send.at[p],
+            recv_sem=e_recv.at[p],
+            device_id={"col": help_col},
+            device_id_type=MESH,
+        )
+
+    def x_copy(p, o):
+        rows = pl.ds(p * piece, piece)
+        return pltpu.make_async_remote_copy(
+            src_ref=tg2.at[row, rows],
+            dst_ref=tg2.at[row, rows],
+            send_sem=x_send.at[p, o - 1],
+            recv_sem=x_recv.at[p, o - 1],
+            device_id={"row": row_peer(o)},
+            device_id_type=MESH,
+        )
+
+    def take(p):
+        e_copy(p).wait_recv()
+        if gathered:
+            plain(tg2, 1, p, p + 1)
+        else:
+            for o in range(1, n_row):
+                x_copy(p, o).start()
+            place(tg2, 1, row, p, p + 1)
+
+    def take_peers(p):
+        if not gathered:
+            for o in range(1, n_row):
+                x_copy(p, o).wait_recv()
+                place(tg2, 1, (row + n_row - o) % n_row, p, p + 1)
 
     t_own.wait()
     if not gathered:
-        place(row)
+        place(tg, 0, row, 0, n_depth)
     else:
-        def body(m, c):
-            at = pl.ds(pl.multiple_of(m * 64, 64), 64)
-            th[at, :], tl[at, :] = halves(tg[at, :])
-            return c
-
-        lax.fori_loop(0, rows_all // 64, body, 0)
+        plain(tg, 0, 0, n_depth)
+
+    def goes_right(b):
+        return (col < n_col - 1) & ((b > 0) | (col < n_col - 2))
+
+    def goes_left(b):
+        return (col > 0) & ((b < n_col - 1) | (col > 1))
 
     def forward(b, h):
         w_copy(wg, b, h, 0).wait_recv()
 
-        @pl.when((b < col) & (col < n_col - 1))
+        @pl.when((b < col) & goes_right(b))
         def _():
             w_copy(wg, b, h, 1).start()
 
-        @pl.when((b > col) & (col > 0))
+        @pl.when((b > col) & goes_left(b))
         def _():
             w_copy(wg, b, h, 0).start()
 
@@ -162,8 +233,13 @@
     if not gathered:
         for o in range(1, n_row):
             t_copy(o).wait_recv()
-            place((row + n_row - o) % n_row)
+            place(tg, 0, (row + n_row - o) % n_row, 0, n_depth)
     w_own.wait()
+
+    @pl.when(at_end)
+    def _():
+        for p in range(n_depth):
+            e_copy(p).start()
 
     near = jnp.minimum(col, n_col - 1 - col)
 
@@ -173,7 +249,7 @@
         s = jnp.where(both, (p + 1) // 2, p - near)
         left = jnp.where(both, p % 2 == 1, col > near)
         b = jnp.where(p == 0, col, jnp.where(left, col - s, col + s))
-        return b, h, s
+        return jnp.where(p < n_col, b, far), h, s
 
     def s1_copy(k):
         return pltpu.make_async_remote_copy(
@@ -209,15 +285,45 @@
             device_id_type=MESH,
         )
 
+    def d_copy(k, o):
+        h = k % n_ch
+        return pltpu.make_async_remote_copy(
+            src_ref=fin.at[k, pl.ds(pl.multiple_of(row_peer(o) * rows_r, rows_r), rows_r)],
+            dst_ref=out_ref.at[:, out_cols(k)],
+            send_sem=d_send.at[h, o],
+            recv_sem=d_recv.at[h, o],
+            device_id={"row": row_peer(o), "col": end_col},
+            device_id_type=MESH,
+        )
+
     def dot(a, b):
         return lax.dot_general(a, b, (((1,), (1,)), ((), ())), preferred_element_type=jnp.float32)
 
     def step(k, c):
-        @pl.when(k < steps)
+        h_now = k % n_ch
+        per_h = n_depth // n_ch
+
+        @pl.when(helps & (k >= steps - n_ch) & (k < steps))
+        def _():
+            for p in range(per_h):
+
+                @pl.when(h_now > 0)
+                def _():
+                    take_peers((h_now - 1) * per_h + p)
+
+                take(h_now * per_h + p)
+
+        @pl.when(helps & (k == steps))
+        def _():
+            for p in range(per_h):
+                take_peers((n_ch - 1) * per_h + p)
+
+        @pl.when(k < total_steps)
         def _():
             b, h, s = block_at(k)
-
-            @pl.when(s >= 2)
+            which = jnp.where(k < steps, 0, 1)
+
+            @pl.when((s >= 2) & (k < steps))
             def _():
                 forward(b, h)
 
@@ -225,11 +331,11 @@
             tile = rows_all // 2
             for m in range(2):
                 at = pl.ds(m * tile, tile)
-                a = th[at, :]
-                part[k, at, :] = dot(a, wh) + dot(a, wl) + dot(tl[at, :], wh)
+                a = th[which, at, :]
+                part[k, at, :] = dot(a, wh) + dot(a, wl) + dot(tl[which, at, :], wh)
             s1_copy(k).start()
 
-        @pl.when((k >= 1) & (k < steps + 1))
+        @pl.when((k >= 1) & (k < total_steps + 1))
         def _():
             j = k - 1
             s1_copy(j).wait_recv()
@@ -246,34 +352,73 @@
                 s2_copy(j, o).wait_recv()
                 total = total + recv2[j, o - 1]
             fin[j] = total
-            for o in range(1, n_row):
-                r_copy(j, o).start()
-            out_ref[:, out_cols(j)] = fin[j, pl.ds(pl.multiple_of(row * rows_r, rows_r), rows_r), :]
+
+            @pl.when(j < normal)
+            def _():
+                for o in range(1, n_row):
+                    r_copy(j, o).start()
+                out_ref[:, out_cols(j)] = fin[j, pl.ds(pl.multiple_of(row * rows_r, rows_r), rows_r), :]
+
+            @pl.when(j >= normal)
+            def _():
+                for o in range(n_row):
+                    d_copy(j, o).start()
 
         return c
 
-    lax.fori_loop(0, steps + 2, step, 0)
+    lax.fori_loop(0, total_steps + 2, step, 0)
 
     def drain(k, c):
         s1_copy(k).wait_send()
         for o in range(1, n_hi):
             s2_copy(k, o).wait_send()
-        for o in range(1, n_row):
-            r_copy(k, o).wait_send()
-            r_copy(k, o).wait_recv()
+
+        @pl.when(k < normal)
+        def _():
+            for o in range(1, n_row):
+                r_copy(k, o).wait_send()
+                r_copy(k, o).wait_recv()
+
+        @pl.when(k >= normal)
+        def _():
+            for o in range(n_row):
+                d_copy(k, o).wait_send()
+
+        return c
+
+    lax.fori_loop(0, total_steps, drain, 0)
+
+    def drain_w(k, c):
         b, h = k // n_ch, k % n_ch
 
-        @pl.when((b <= col) & (col < n_col - 1))
+        @pl.when((b <= col) & goes_right(b))
         def _():
             w_copy(wg, b, h, 1).wait_send()
 
-        @pl.when((b >= col) & (col > 0))
+        @pl.when((b >= col) & goes_left(b))
         def _():
             w_copy(wg, b, h, 0).wait_send()
 
         return c
 
-    lax.fori_loop(0, steps, drain, 0)
+    lax.fori_loop(0, steps, drain_w, 0)
+
+    @pl.when(at_end)
+    def _():
+        for p in range(n_depth):
+            e_copy(p).wait_send()
+        for h in range(n_ch):
+            for o in range(n_row):
+                d_copy(h, o).wait_recv()
+
+    if not gathered:
+
+        @pl.when(helps)
+        def _():
+            for p in range(n_depth):
+                for o in range(1, n_row):
+                    x_copy(p, o).wait_send()
+
     if not gathered:
         for o in range(1, n_row):
             t_copy(o).wait_send()
@@ -286,7 +431,8 @@
     kc, i_count, j_local = amplitudes.shape
     j_count = j_local * n_row
     ab_rows = integrals.shape[0]
-    steps = n_col * (ab_rows // CHUNK)
+    n_ch = ab_rows // CHUNK
+    slots = (n_col + 1) * n_ch
     rows_all = i_count * j_count
     rows_lo = rows_all // n_lo
     rows_d = rows_lo // n_hi
@@ -314,23 +460,30 @@
         scratch_shapes=[
             pltpu.VMEM((n_col, ab_rows, kc), jnp.float32),
             tg,
-            pltpu.VMEM((rows_all, kc), jnp.bfloat16),
-            pltpu.VMEM((rows_all, kc), jnp.bfloat16),
-            pltpu.VMEM((steps, rows_all, CHUNK), jnp.float32),
-            pltpu.VMEM((steps, rows_lo, CHUNK), jnp.float32),
-            pltpu.VMEM((steps, max(n_hi - 1, 1), rows_d, CHUNK), jnp.float32),
-            pltpu.VMEM((steps, rows_d, CHUNK), jnp.float32),
+            tg,
+            pltpu.VMEM((2, rows_all, kc), jnp.bfloat16),
+            pltpu.VMEM((2, rows_all, kc), jnp.bfloat16),
+            pltpu.VMEM((slots, rows_all, CHUNK), jnp.float32),
+            pltpu.VMEM((slots, rows_lo, CHUNK), jnp.float32),
+            pltpu.VMEM((slots, max(n_hi - 1, 1), rows_d, CHUNK), jnp.float32),
+            pltpu.VMEM((slots, rows_d, CHUNK), jnp.float32),
             dma((2,)),
             dma((2, n_col, ab_rows // CHUNK)),
             dma((n_col, ab_rows // CHUNK)),
             dma((max(n_row - 1, 1),)),
             dma((max(n_row - 1, 1),)),
-            dma((steps,)),
-            dma((steps,)),
-            dma((steps, max(n_hi - 1, 1))),
-            dma((steps, max(n_hi - 1, 1))),
-            dma((steps, max(n_row - 1, 1))),
-            dma((steps, max(n_row - 1, 1))),
+            dma((slots,)),
+            dma((slots,)),
+            dma((slots, max(n_hi - 1, 1))),
+            dma((slots, max(n_hi - 1, 1))),
+            dma((slots, max(n_row - 1, 1))),
+            dma((slots, max(n_row - 1, 1))),
+            dma((n_depth,)),
+            dma((n_depth,)),
+            dma((n_depth, max(n_row - 1, 1))),
+            dma((n_depth, max(n_row - 1, 1))),
+            dma((n_ch, n_row)),
+            dma((n_ch, n_row)),
         ],
         compiler_params=pltpu.CompilerParams(
             collective_id=0, has_side_effects=True, vmem_limit_bytes=60 * 2**20

time: 165 us -> 168 us (1.018)
  Pallas kernels: 162 us -> 165 us
    pallas_call x1, Pallas kernels: 162 us -> 165 us  [shards(): pl.pallas_call(functools.partial(kernel, sizes, gathered), out_shape=jax....]
where the time goes in v2:
time: 168 us
  Pallas kernels  165 us (98%)
  local copies, waits for them, and re-layouts  3.11 us (2%)
    pallas_call x1, Pallas kernels, shards(): pl.pallas_call(functools.partial(kernel, sizes, gathered), out_shape=jax....  165 us

profile of v2, /device:TPU:0, one launch (start us, length us, event | category | flops | bytes accessed | tf_op | source)
XLA Modules:
  0.0 168.0 jit_solution(7879644765641357832)
XLA Ops:
  0.0 164.9 %shard_map.37 = f32[128,4096]{1,0:T(8,128)} custom-call(f32[512,1024]{1,0:T(8,128)} %w_ref.1, f32[16,32,1024]{2,1,0:T(8,128)} %bitcast.3, bf16[128,128]{1,0:T(8,128)(2,1)} %constant.2.clone.order_ref), custom_call_target="tpu_custom_call" | custom-call | flops 12884901888 | bytes 6291456 | tf_op jit(solution)/shard_map/pallas_call | solution.py:455
  164.9 3.1 %copy.5 = f32[4,32,4096]{2,1,0:T(8,128)} copy(f32[4,32,4096]{2,1,0:T(8,128)} %bitcast.2) | data formatting | bytes 4194304

commit v3 on v2

--- a/solution.py
+++ b/solution.py
@@ -27,6 +27,7 @@
     n_hi = n_depth // n_lo
     ab_rows = w_ref.shape[0]
     n_ch = ab_rows // CHUNK
+    assert n_ch == 2 and n_depth == 4 and n_col == 4
     steps = n_col * n_ch
     rows_all = th.shape[1]
     rows_lo = rows_all // n_lo
@@ -96,18 +97,40 @@
             device_id_type=MESH,
         )
 
-    def send_own(h, c):
+    def own_sends(act, h):
         @pl.when(col > 0)
         def _():
-            w_copy(None, col, h, 0).start()
+            getattr(w_copy(None, col, h, 0), act)()
 
         @pl.when(col < n_col - 1)
         def _():
-            w_copy(None, col, h, 1).start()
-
-        return c
-
-    lax.fori_loop(0, n_ch, send_own, 0)
+            getattr(w_copy(None, col, h, 1), act)()
+
+    def near_sends(act, h):
+        @pl.when((col > 0) & goes_right(col - 1))
+        def _():
+            getattr(w_copy(wg, col - 1, h, 1), act)()
+
+        @pl.when((col < n_col - 1) & goes_left(col + 1))
+        def _():
+            getattr(w_copy(wg, col + 1, h, 0), act)()
+
+    def near_arrive(h):
+        @pl.when(col > 0)
+        def _():
+            w_copy(wg, col - 1, h, 0).wait_recv()
+
+        @pl.when(col < n_col - 1)
+        def _():
+            w_copy(wg, col + 1, h, 0).wait_recv()
+
+    def goes_right(b):
+        return (col < n_col - 1) & ((b > 0) | (col < n_col - 2))
+
+    def goes_left(b):
+        return (col > 0) & ((b < n_col - 1) | (col > 1))
+
+    own_sends("start", 0)
 
     def t_copy(o):
         return pltpu.make_async_remote_copy(
@@ -200,46 +223,22 @@
     else:
         plain(tg, 0, 0, n_depth)
 
-    def goes_right(b):
-        return (col < n_col - 1) & ((b > 0) | (col < n_col - 2))
-
-    def goes_left(b):
-        return (col > 0) & ((b < n_col - 1) | (col > 1))
-
-    def forward(b, h):
-        w_copy(wg, b, h, 0).wait_recv()
-
-        @pl.when((b < col) & goes_right(b))
-        def _():
-            w_copy(wg, b, h, 1).start()
-
-        @pl.when((b > col) & goes_left(b))
-        def _():
-            w_copy(wg, b, h, 0).start()
-
-    def first(h, c):
-        @pl.when(col > 0)
-        def _():
-            forward(col - 1, h)
-
-        @pl.when(col < n_col - 1)
-        def _():
-            forward(col + 1, h)
-
-        return c
-
-    lax.fori_loop(0, n_ch, first, 0)
-
+    own_sends("wait_send", 0)
+    own_sends("start", 1)
+    near_arrive(0)
+    own_sends("wait_send", 1)
+    near_sends("start", 0)
+
+    @pl.when(at_end)
+    def _():
+        e_copy(0).start()
+
+    near_arrive(1)
     if not gathered:
         for o in range(1, n_row):
             t_copy(o).wait_recv()
             place(tg, 0, (row + n_row - o) % n_row, 0, n_depth)
     w_own.wait()
-
-    @pl.when(at_end)
-    def _():
-        for p in range(n_depth):
-            e_copy(p).start()
 
     near = jnp.minimum(col, n_col - 1 - col)
 
@@ -323,9 +322,32 @@
             b, h, s = block_at(k)
             which = jnp.where(k < steps, 0, 1)
 
+            late = k - (normal - n_ch)
+
+            @pl.when(at_end & (late == 0))
+            def _():
+                e_copy(0).wait_send()
+                e_copy(1).start()
+
+            @pl.when(at_end & (late == 1))
+            def _():
+                e_copy(2).wait_send()
+                e_copy(3).start()
+
             @pl.when((s >= 2) & (k < steps))
             def _():
-                forward(b, h)
+                w_copy(wg, b, h, 0).wait_recv()
+
+            @pl.when(late == 0)
+            def _():
+                near_sends("wait_send", 0)
+                near_sends("start", 1)
+
+                @pl.when(at_end)
+                def _():
+                    e_copy(1).wait_send()
+                    e_copy(2).start()
+
 
             wh, wl = halves(wg[b, pl.ds(pl.multiple_of(h * CHUNK, CHUNK), CHUNK), :])
             tile = rows_all // 2
@@ -388,25 +410,11 @@
 
     lax.fori_loop(0, total_steps, drain, 0)
 
-    def drain_w(k, c):
-        b, h = k // n_ch, k % n_ch
-
-        @pl.when((b <= col) & goes_right(b))
-        def _():
-            w_copy(wg, b, h, 1).wait_send()
-
-        @pl.when((b >= col) & goes_left(b))
-        def _():
-            w_copy(wg, b, h, 0).wait_send()
-
-        return c
-
-    lax.fori_loop(0, steps, drain_w, 0)
+    near_sends("wait_send", 1)
 
     @pl.when(at_end)
     def _():
-        for p in range(n_depth):
-            e_copy(p).wait_send()
+        e_copy(3).wait_send()
         for h in range(n_ch):
             for o in range(n_row):
                 d_copy(h, o).wait_recv()

time: 168 us -> 168 us (level)
  no operation moved by 1% of the time
where the time goes in v3:
time: 168 us
  Pallas kernels  165 us (98%)
  local copies, waits for them, and re-layouts  3.11 us (2%)
    pallas_call x1, Pallas kernels, shards(): pl.pallas_call(functools.partial(kernel, sizes, gathered), out_shape=jax....  165 us

profile of v3, /device:TPU:0, one launch (start us, length us, event | category | flops | bytes accessed | tf_op | source)
XLA Modules:
  0.0 167.9 jit_solution(2015786102356725964)
XLA Ops:
  0.0 164.8 %shard_map.37 = f32[128,4096]{1,0:T(8,128)} custom-call(f32[512,1024]{1,0:T(8,128)} %w_ref.1, f32[16,32,1024]{2,1,0:T(8,128)} %bitcast.3, bf16[128,128]{1,0:T(8,128)(2,1)} %constant.2.clone.order_ref), custom_call_target="tpu_custom_call" | custom-call | flops 12884901888 | bytes 6291456 | tf_op jit(solution)/shard_map/pallas_call | solution.py:463
  164.8 3.1 %copy.5 = f32[4,32,4096]{2,1,0:T(8,128)} copy(f32[4,32,4096]{2,1,0:T(8,128)} %bitcast.2) | data formatting | bytes 4194304

commit v4 on v3

--- a/solution.py
+++ b/solution.py
@@ -204,14 +204,17 @@
 
     def take(p):
         e_copy(p).wait_recv()
+        if not gathered:
+            for o in range(1, n_row):
+                x_copy(p, o).start()
+
+    def place_own(p):
         if gathered:
             plain(tg2, 1, p, p + 1)
         else:
-            for o in range(1, n_row):
-                x_copy(p, o).start()
             place(tg2, 1, row, p, p + 1)
 
-    def take_peers(p):
+    def place_peers(p):
         if not gathered:
             for o in range(1, n_row):
                 x_copy(p, o).wait_recv()
@@ -232,6 +235,7 @@
     @pl.when(at_end)
     def _():
         e_copy(0).start()
+        e_copy(1).start()
 
     near_arrive(1)
     if not gathered:
@@ -295,66 +299,60 @@
             device_id_type=MESH,
         )
 
-    def dot(a, b):
-        return lax.dot_general(a, b, (((1,), (1,)), ((), ())), preferred_element_type=jnp.float32)
-
     def step(k, c):
-        h_now = k % n_ch
-        per_h = n_depth // n_ch
-
-        @pl.when(helps & (k >= steps - n_ch) & (k < steps))
-        def _():
-            for p in range(per_h):
-
-                @pl.when(h_now > 0)
-                def _():
-                    take_peers((h_now - 1) * per_h + p)
-
-                take(h_now * per_h + p)
+        @pl.when(helps & (k == steps - 4))
+        def _():
+            take(0)
+
+        @pl.when(helps & (k == steps - 3))
+        def _():
+            take(1)
+
+        @pl.when(helps & (k == steps - 1))
+        def _():
+            place_own(0)
+            place_own(1)
+            place_peers(0)
+            take(2)
+            place_own(2)
+            take(3)
+            place_own(3)
 
         @pl.when(helps & (k == steps))
         def _():
-            for p in range(per_h):
-                take_peers((n_ch - 1) * per_h + p)
+            for p in range(1, n_depth):
+                place_peers(p)
+
+        @pl.when(k == normal - 3)
+        def _():
+            near_sends("wait_send", 0)
+            near_sends("start", 1)
+
+        @pl.when(at_end & (k == normal - 2))
+        def _():
+            e_copy(0).wait_send()
+            e_copy(1).wait_send()
+            e_copy(2).start()
+            e_copy(3).start()
 
         @pl.when(k < total_steps)
         def _():
             b, h, s = block_at(k)
             which = jnp.where(k < steps, 0, 1)
-
-            late = k - (normal - n_ch)
-
-            @pl.when(at_end & (late == 0))
-            def _():
-                e_copy(0).wait_send()
-                e_copy(1).start()
-
-            @pl.when(at_end & (late == 1))
-            def _():
-                e_copy(2).wait_send()
-                e_copy(3).start()
 
             @pl.when((s >= 2) & (k < steps))
             def _():
                 w_copy(wg, b, h, 0).wait_recv()
 
-            @pl.when(late == 0)
-            def _():
-                near_sends("wait_send", 0)
-                near_sends("start", 1)
-
-                @pl.when(at_end)
-                def _():
-                    e_copy(1).wait_send()
-                    e_copy(2).start()
-
-
-            wh, wl = halves(wg[b, pl.ds(pl.multiple_of(h * CHUNK, CHUNK), CHUNK), :])
+            w_t = wg[b, pl.ds(pl.multiple_of(h * CHUNK, CHUNK), CHUNK), :].T
+            wh, wl = halves(w_t)
+            w3 = jnp.concatenate([wh, wh, wl], axis=0)
             tile = rows_all // 2
             for m in range(2):
                 at = pl.ds(m * tile, tile)
                 a = th[which, at, :]
-                part[k, at, :] = dot(a, wh) + dot(a, wl) + dot(tl[which, at, :], wh)
+                a3 = jnp.concatenate([a, tl[which, at, :], a], axis=1)
+                part[k, at, :] = jnp.dot(a3, w3, preferred_element_type=jnp.float32)
             s1_copy(k).start()
 
         @pl.when((k >= 1) & (k < total_steps + 1))
@@ -414,6 +412,7 @@
 
     @pl.when(at_end)
     def _():
+        e_copy(2).wait_send()
         e_copy(3).wait_send()
         for h in range(n_ch):
             for o in range(n_row):

time: 168 us -> 163 us (0.970)
  Pallas kernels: 165 us -> 159 us
    pallas_call x1, Pallas kernels: 165 us -> 159 us  [shards(): pl.pallas_call(functools.partial(kernel, sizes, gathered), out_shape=jax....]
where the time goes in v4:
time: 163 us; the launch traced here: 162 us
  Pallas kernels  159 us (98%)
  local copies, waits for them, and re-layouts  3.11 us (2%)
    pallas_call x1, Pallas kernels, shards(): pl.pallas_call(functools.partial(kernel, sizes, gathered), out_shape=jax....  159 us

profile of v4, /device:TPU:0, one launch (start us, length us, event | category | flops | bytes accessed | tf_op | source)
XLA Modules:
  0.0 162.3 jit_solution(6782547869059240689)
XLA Ops:
  0.0 159.2 %shard_map.37 = f32[128,4096]{1,0:T(8,128)} custom-call(f32[512,1024]{1,0:T(8,128)} %w_ref.1, f32[16,32,1024]{2,1,0:T(8,128)} %bitcast.3, bf16[128,128]{1,0:T(8,128)(2,1)} %constant.2.clone.order_ref), custom_call_target="tpu_custom_call" | custom-call | flops 12884901888 | bytes 6291456 | tf_op jit(solution)/shard_map/pallas_call | solution.py:462
  159.2 3.1 %copy.5 = f32[4,32,4096]{2,1,0:T(8,128)} copy(f32[4,32,4096]{2,1,0:T(8,128)} %bitcast.2) | data formatting | bytes 4194304

commit v5 on v4

--- a/solution.py
+++ b/solution.py
@@ -21,7 +21,7 @@
 
 def kernel(sizes, gathered, w_ref, t_ref, order_ref, out_ref, wg, tg, tg2, th, tl, part, recv1, recv2, fin,
            own_sem, w_send, w_recv, t_send, t_recv, s1_send, s1_recv, s2_send, s2_recv, r_send, r_recv,
-           e_send, e_recv, x_send, x_recv, d_send, d_recv):
+           e_send, e_recv, f_send, f_recv, x_send, x_recv, d_send, d_recv):
     n_row, n_col, n_depth = sizes
     n_lo = LANES
     n_hi = n_depth // n_lo
@@ -179,6 +179,7 @@
         lax.fori_loop(first * (rows_all // 64) // n_depth, last * (rows_all // 64) // n_depth, body, 0)
 
     piece = t_ref.shape[0] // n_depth
+    n_swap = n_depth // 2
 
     def e_copy(p):
         rows = pl.ds(p * piece, piece)
@@ -202,9 +203,21 @@
             device_id_type=MESH,
         )
 
+    def f_copy(p, o):
+        q = (row + n_row - o) % n_row
+        rows = pl.ds(p * piece, piece)
+        return pltpu.make_async_remote_copy(
+            src_ref=tg.at[q, rows],
+            dst_ref=tg2.at[q, rows],
+            send_sem=f_send.at[p, o - 1],
+            recv_sem=f_recv.at[p, o - 1],
+            device_id={"col": help_col},
+            device_id_type=MESH,
+        )
+
     def take(p):
         e_copy(p).wait_recv()
-        if not gathered:
+        if not gathered and p < n_swap:
             for o in range(1, n_row):
                 x_copy(p, o).start()
 
@@ -217,7 +230,7 @@
     def place_peers(p):
         if not gathered:
             for o in range(1, n_row):
-                x_copy(p, o).wait_recv()
+                (x_copy if p < n_swap else f_copy)(p, o).wait_recv()
                 place(tg2, 1, (row + n_row - o) % n_row, p, p + 1)
 
     t_own.wait()
@@ -313,14 +326,13 @@
             place_own(0)
             place_own(1)
             place_peers(0)
-            take(2)
-            place_own(2)
-            take(3)
-            place_own(3)
 
         @pl.when(helps & (k == steps))
         def _():
-            for p in range(1, n_depth):
+            place_peers(1)
+            for p in range(n_swap, n_depth):
+                take(p)
+                place_own(p)
                 place_peers(p)
 
         @pl.when(k == normal - 3)
@@ -328,12 +340,15 @@
             near_sends("wait_send", 0)
             near_sends("start", 1)
 
-        @pl.when(at_end & (k == normal - 2))
-        def _():
-            e_copy(0).wait_send()
-            e_copy(1).wait_send()
-            e_copy(2).start()
-            e_copy(3).start()
+        @pl.when(at_end & (k == normal - 3))
+        def _():
+            for p in range(n_swap):
+                e_copy(p).wait_send()
+            for p in range(n_swap, n_depth):
+                e_copy(p).start()
+                if not gathered:
+                    for o in range(1, n_row):
+                        f_copy(p, o).start()
 
         @pl.when(k < total_steps)
         def _():
@@ -412,8 +427,11 @@
 
     @pl.when(at_end)
     def _():
-        e_copy(2).wait_send()
-        e_copy(3).wait_send()
+        for p in range(n_swap, n_depth):
+            e_copy(p).wait_send()
+            if not gathered:
+                for o in range(1, n_row):
+                    f_copy(p, o).wait_send()
         for h in range(n_ch):
             for o in range(n_row):
                 d_copy(h, o).wait_recv()
@@ -422,7 +440,7 @@
 
         @pl.when(helps)
         def _():
-            for p in range(n_depth):
+            for p in range(n_swap):
                 for o in range(1, n_row):
                     x_copy(p, o).wait_send()
 
@@ -489,6 +507,8 @@
             dma((n_depth,)),
             dma((n_depth, max(n_row - 1, 1))),
             dma((n_depth, max(n_row - 1, 1))),
+            dma((n_depth, max(n_row - 1, 1))),
+            dma((n_depth, max(n_row - 1, 1))),
             dma((n_ch, n_row)),
             dma((n_ch, n_row)),
         ],

time: 163 us -> 151 us (0.926)
  Pallas kernels: 159 us -> 148 us
    pallas_call x1, Pallas kernels: 159 us -> 148 us  [shards(): pl.pallas_call(functools.partial(kernel, sizes, gathered), out_shape=jax....]
where the time goes in v5:
time: 151 us
  Pallas kernels  148 us (98%)
  local copies, waits for them, and re-layouts  3.11 us (2%)
    pallas_call x1, Pallas kernels, shards(): pl.pallas_call(functools.partial(kernel, sizes, gathered), out_shape=jax....  148 us
    unnamed x1, local copies, waits for them, and re-layouts  3.11 us

profile of v5, /device:TPU:0, one launch (start us, length us, event | category | flops | bytes accessed | tf_op | source)
XLA Modules:
  0.0 150.6 jit_solution(11522459354782627609)
XLA Ops:
  0.0 147.5 %shard_map.37 = f32[128,4096]{1,0:T(8,128)} custom-call(f32[512,1024]{1,0:T(8,128)} %w_ref.1, f32[16,32,1024]{2,1,0:T(8,128)} %bitcast.3, bf16[128,128]{1,0:T(8,128)(2,1)} %constant.2.clone.order_ref), custom_call_target="tpu_custom_call" | custom-call | flops 12884901888 | bytes 6291456 | tf_op jit(solution)/shard_map/pallas_call | solution.py:480
  147.5 3.1 %copy.5 = f32[4,32,4096]{2,1,0:T(8,128)} copy(f32[4,32,4096]{2,1,0:T(8,128)} %bitcast.2) | data formatting | bytes 4194304

commit v6 on v5

--- a/solution.py
+++ b/solution.py
@@ -20,8 +20,9 @@
 
 
 def kernel(sizes, gathered, w_ref, t_ref, order_ref, out_ref, wg, tg, tg2, th, tl, part, recv1, recv2, fin,
+           part_d, recv1_d, recv2_d, fin_d,
            own_sem, w_send, w_recv, t_send, t_recv, s1_send, s1_recv, s2_send, s2_recv, r_send, r_recv,
-           e_send, e_recv, f_send, f_recv, x_send, x_recv, d_send, d_recv):
+           e_send, e_recv, f_send, f_recv, x_send, x_recv, d1_send, d1_recv, d2_send, d2_recv, d_send, d_recv):
     n_row, n_col, n_depth = sizes
     n_lo = LANES
     n_hi = n_depth // n_lo
@@ -49,7 +50,6 @@
     end_col = jnp.where(col < n_col // 2, 0, n_col - 1)
     help_col = jnp.where(col < n_col // 2, 1, n_col - 2)
     normal = jnp.where(at_end, steps - n_ch, steps)
-    total_steps = jnp.where(helps, steps + n_ch, normal)
 
     barrier = pltpu.get_barrier_semaphore()
     for o in range(1, n_row):
@@ -152,40 +152,59 @@
     w_own = pltpu.make_async_copy(w_ref, wg.at[col], own_sem.at[0])
     w_own.start()
 
-    def place(src, which, q, first, last):
-        i_count, j_local, kc = t_ref.shape
-        i_out = i_count // n_depth
+    def place(src, q):
+        i_out, j_local, kc = t_ref.shape[1:]
         per_r = j_local // n_row
         order = order_ref[...]
 
         def body(d, c):
-            x = src[q, pl.ds(d * i_out, i_out)].reshape(i_out * j_local, kc)
+            x = src[q, d].reshape(i_out * j_local, kc)
             base = (d % n_lo) * rows_lo + (d // n_lo) * rows_d
             for x_part, into in zip(halves(x), (th, tl)):
                 y = jnp.dot(order, x_part, preferred_element_type=jnp.float32).astype(jnp.bfloat16)
-                for piece in range(n_row * i_out):
-                    at = base + piece * (per_r * n_row) + q * per_r
-                    into[which, pl.ds(pl.multiple_of(at, per_r), per_r), :] = y[piece * per_r : (piece + 1) * per_r]
+                for n in range(n_row * i_out):
+                    at = base + n * (per_r * n_row) + q * per_r
+                    into[0, pl.ds(pl.multiple_of(at, per_r), per_r), :] = y[n * per_r : (n + 1) * per_r]
             return c
 
-        lax.fori_loop(first, last, body, 0)
-
-    def plain(src, which, first, last):
+        lax.fori_loop(0, n_depth, body, 0)
+
+    def place_piece(q, p):
+        i_out, j_local, kc = t_ref.shape[1:]
+        per_r = j_local // n_row
+        x = tg2[q, :, p].reshape(n_depth * j_local, kc)
+        for x_part, into in zip(halves(x), (th, tl)):
+            y = jnp.dot(order_ref[...], x_part, preferred_element_type=jnp.float32).astype(jnp.bfloat16)
+            for n in range(n_row * n_depth):
+                r, d = n // n_depth, n % n_depth
+                base = (p // 2) * rows_all + (d % n_lo) * rows_lo + (d // n_lo) * rows_d + r * rows_r
+                at = base // 2 + (p % 2) * (per_r * n_row) + q * per_r
+                into[1, pl.ds(pl.multiple_of(at, per_r), per_r), :] = y[n * per_r : (n + 1) * per_r]
+
+    def plain_groups():
+        for d in range(n_depth):
+            base = (d % n_lo) * rows_lo + (d // n_lo) * rows_d
+            x = tg2[pl.ds(base, rows_d), :].reshape(n_row, 2, rows_r // 2, -1)
+            for g in range(2):
+                at = pl.ds((g * rows_all + base) // 2, rows_d // 2)
+                th[1, at, :], tl[1, at, :] = halves(x[:, g].reshape(rows_d // 2, -1))
+
+    def plain():
         def body(m, c):
             at = pl.ds(pl.multiple_of(m * 64, 64), 64)
-            th[which, at, :], tl[which, at, :] = halves(src[at, :])
+            th[0, at, :], tl[0, at, :] = halves(tg[at, :])
             return c
 
-        lax.fori_loop(first * (rows_all // 64) // n_depth, last * (rows_all // 64) // n_depth, body, 0)
-
-    piece = t_ref.shape[0] // n_depth
+        lax.fori_loop(0, rows_all // 64, body, 0)
+
+    piece = rows_all // n_depth
     n_swap = n_depth // 2
 
     def e_copy(p):
         rows = pl.ds(p * piece, piece)
         return pltpu.make_async_remote_copy(
-            src_ref=t_ref.at[rows],
-            dst_ref=tg2.at[rows] if gathered else tg2.at[row, rows],
+            src_ref=t_ref.at[rows] if gathered else t_ref.at[:, p],
+            dst_ref=tg2.at[rows] if gathered else tg2.at[row, :, p],
             send_sem=e_send.at[p],
             recv_sem=e_recv.at[p],
             device_id={"col": help_col},
@@ -193,10 +212,9 @@
         )
 
     def x_copy(p, o):
-        rows = pl.ds(p * piece, piece)
-        return pltpu.make_async_remote_copy(
-            src_ref=tg2.at[row, rows],
-            dst_ref=tg2.at[row, rows],
+        return pltpu.make_async_remote_copy(
+            src_ref=tg2.at[row, :, p],
+            dst_ref=tg2.at[row, :, p],
             send_sem=x_send.at[p, o - 1],
             recv_sem=x_recv.at[p, o - 1],
             device_id={"row": row_peer(o)},
@@ -205,10 +223,9 @@
 
     def f_copy(p, o):
         q = (row + n_row - o) % n_row
-        rows = pl.ds(p * piece, piece)
-        return pltpu.make_async_remote_copy(
-            src_ref=tg.at[q, rows],
-            dst_ref=tg2.at[q, rows],
+        return pltpu.make_async_remote_copy(
+            src_ref=tg.at[q, :, p],
+            dst_ref=tg2.at[q, :, p],
             send_sem=f_send.at[p, o - 1],
             recv_sem=f_recv.at[p, o - 1],
             device_id={"col": help_col},
@@ -222,22 +239,20 @@
                 x_copy(p, o).start()
 
     def place_own(p):
-        if gathered:
-            plain(tg2, 1, p, p + 1)
-        else:
-            place(tg2, 1, row, p, p + 1)
+        if not gathered:
+            place_piece(row, p)
 
     def place_peers(p):
         if not gathered:
             for o in range(1, n_row):
                 (x_copy if p < n_swap else f_copy)(p, o).wait_recv()
-                place(tg2, 1, (row + n_row - o) % n_row, p, p + 1)
+                place_piece((row + n_row - o) % n_row, p)
 
     t_own.wait()
     if not gathered:
-        place(tg, 0, row, 0, n_depth)
+        place(tg, row)
     else:
-        plain(tg, 0, 0, n_depth)
+        plain()
 
     own_sends("wait_send", 0)
     own_sends("start", 1)
@@ -254,7 +269,7 @@
     if not gathered:
         for o in range(1, n_row):
             t_copy(o).wait_recv()
-            place(tg, 0, (row + n_row - o) % n_row, 0, n_depth)
+            place(tg, (row + n_row - o) % n_row)
     w_own.wait()
 
     near = jnp.minimum(col, n_col - 1 - col)
@@ -265,7 +280,7 @@
         s = jnp.where(both, (p + 1) // 2, p - near)
         left = jnp.where(both, p % 2 == 1, col > near)
         b = jnp.where(p == 0, col, jnp.where(left, col - s, col + s))
-        return jnp.where(p < n_col, b, far), h, s
+        return b, h, s
 
     def s1_copy(k):
         return pltpu.make_async_remote_copy(
@@ -287,30 +302,101 @@
             device_id_type=MESH,
         )
 
-    def out_cols(k):
-        b, h, _ = block_at(k)
+    def out_cols(b, h):
         return pl.ds(pl.multiple_of((row * n_col + b) * ab_rows + h * CHUNK, CHUNK), CHUNK)
 
     def r_copy(k, o):
         return pltpu.make_async_remote_copy(
             src_ref=fin.at[k, pl.ds(pl.multiple_of(row_peer(o) * rows_r, rows_r), rows_r)],
-            dst_ref=out_ref.at[:, out_cols(k)],
+            dst_ref=out_ref.at[:, out_cols(*block_at(k)[:2])],
             send_sem=r_send.at[k, o - 1],
             recv_sem=r_recv.at[k, o - 1],
             device_id={"row": row_peer(o)},
             device_id_type=MESH,
         )
 
-    def d_copy(k, o):
-        h = k % n_ch
-        return pltpu.make_async_remote_copy(
-            src_ref=fin.at[k, pl.ds(pl.multiple_of(row_peer(o) * rows_r, rows_r), rows_r)],
-            dst_ref=out_ref.at[:, out_cols(k)],
-            send_sem=d_send.at[h, o],
-            recv_sem=d_recv.at[h, o],
+    def d1_copy(n):
+        return pltpu.make_async_remote_copy(
+            src_ref=part_d.at[n, pl.ds(pl.multiple_of((1 - lo) * (rows_lo // 2), rows_lo // 2), rows_lo // 2)],
+            dst_ref=recv1_d.at[n],
+            send_sem=d1_send.at[n],
+            recv_sem=d1_recv.at[n],
+            device_id={"depth": mate},
+            device_id_type=MESH,
+        )
+
+    def d2_copy(n, o):
+        start = lo * (rows_lo // 2) + hi_peer(o) * (rows_d // 2)
+        return pltpu.make_async_remote_copy(
+            src_ref=part_d.at[n, pl.ds(pl.multiple_of(start, rows_d // 2), rows_d // 2)],
+            dst_ref=recv2_d.at[n, o - 1],
+            send_sem=d2_send.at[n, o - 1],
+            recv_sem=d2_recv.at[n, o - 1],
+            device_id={"depth": hi_peer(o) * n_lo + lo},
+            device_id_type=MESH,
+        )
+
+    def d_copy(n, o):
+        g, h = n // n_ch, n % n_ch
+        half = rows_r // 2
+        return pltpu.make_async_remote_copy(
+            src_ref=fin_d.at[n, pl.ds(pl.multiple_of(row_peer(o) * half, half), half)],
+            dst_ref=out_ref.at[pl.ds(g * half, half), out_cols(far, h)],
+            send_sem=d_send.at[n, o],
+            recv_sem=d_recv.at[n, o],
             device_id={"row": row_peer(o), "col": end_col},
             device_id_type=MESH,
         )
+
+    def multiply(b, h, which, first, tile):
+        w_t = wg[b, pl.ds(pl.multiple_of(h * CHUNK, CHUNK), CHUNK), :].T
+        wh, wl = halves(w_t)
+        w3 = jnp.concatenate([wh, wh, wl], axis=0)
+        for start in first:
+            at = pl.ds(start, tile)
+            a = th[which, at, :]
+            a3 = jnp.concatenate([a, tl[which, at, :], a], axis=1)
+            yield start, jnp.dot(a3, w3, preferred_element_type=jnp.float32)
+
+    def d_multiply(n):
+        for _, y in multiply(far, n % n_ch, 1, (n // n_ch * (rows_all // 2),), rows_all // 2):
+            part_d[n] = y
+        d1_copy(n).start()
+
+    def d_pair(n):
+        d1_copy(n).wait_recv()
+        at = pl.ds(pl.multiple_of(lo * (rows_lo // 2), rows_lo // 2), rows_lo // 2)
+        part_d[n, at, :] = part_d[n, at, :] + recv1_d[n]
+        for o in range(1, n_hi):
+            d2_copy(n, o).start()
+
+    def d_finish(n):
+        start = lo * (rows_lo // 2) + hi * (rows_d // 2)
+        total = part_d[n, pl.ds(pl.multiple_of(start, rows_d // 2), rows_d // 2), :]
+        for o in range(1, n_hi):
+            d2_copy(n, o).wait_recv()
+            total = total + recv2_d[n, o - 1]
+        fin_d[n] = total
+        for o in range(n_row):
+            d_copy(n, o).start()
+
+    def pair(j):
+        s1_copy(j).wait_recv()
+        at = pl.ds(pl.multiple_of(lo * rows_lo, rows_lo), rows_lo)
+        part[j, at, :] = part[j, at, :] + recv1[j]
+        for o in range(1, n_hi):
+            s2_copy(j, o).start()
+
+    def finish(j):
+        total = part[j, pl.ds(pl.multiple_of(lo * rows_lo + hi * rows_d, rows_d), rows_d), :]
+        for o in range(1, n_hi):
+            s2_copy(j, o).wait_recv()
+            total = total + recv2[j, o - 1]
+        fin[j] = total
+        for o in range(1, n_row):
+            r_copy(j, o).start()
+        mine = fin[j, pl.ds(pl.multiple_of(row * rows_r, rows_r), rows_r), :]
+        out_ref[:, out_cols(*block_at(j)[:2])] = mine
 
     def step(k, c):
         @pl.when(helps & (k == steps - 4))
@@ -326,14 +412,6 @@
             place_own(0)
             place_own(1)
             place_peers(0)
-
-        @pl.when(helps & (k == steps))
-        def _():
-            place_peers(1)
-            for p in range(n_swap, n_depth):
-                take(p)
-                place_own(p)
-                place_peers(p)
 
         @pl.when(k == normal - 3)
         def _():
@@ -350,78 +428,83 @@
                     for o in range(1, n_row):
                         f_copy(p, o).start()
 
-        @pl.when(k < total_steps)
-        def _():
-            b, h, s = block_at(k)
-            which = jnp.where(k < steps, 0, 1)
-
-            @pl.when((s >= 2) & (k < steps))
-            def _():
-                w_copy(wg, b, h, 0).wait_recv()
-
-            w_t = wg[b, pl.ds(pl.multiple_of(h * CHUNK, CHUNK), CHUNK), :].T
-            wh, wl = halves(w_t)
-            w3 = jnp.concatenate([wh, wh, wl], axis=0)
-            tile = rows_all // 2
-            for m in range(2):
-                at = pl.ds(m * tile, tile)
-                a = th[which, at, :]
-                a3 = jnp.concatenate([a, tl[which, at, :], a], axis=1)
-                part[k, at, :] = jnp.dot(a3, w3, preferred_element_type=jnp.float32)
-            s1_copy(k).start()
-
-        @pl.when((k >= 1) & (k < total_steps + 1))
-        def _():
-            j = k - 1
-            s1_copy(j).wait_recv()
-            at = pl.ds(pl.multiple_of(lo * rows_lo, rows_lo), rows_lo)
-            part[j, at, :] = part[j, at, :] + recv1[j]
-            for o in range(1, n_hi):
-                s2_copy(j, o).start()
+        b, h, s = block_at(k)
+
+        @pl.when(s >= 2)
+        def _():
+            w_copy(wg, b, h, 0).wait_recv()
+
+        for start, y in multiply(b, h, 0, (0, rows_all // 2), rows_all // 2):
+            part[k, pl.ds(start, rows_all // 2), :] = y
+        s1_copy(k).start()
+
+        @pl.when(k >= 1)
+        def _():
+            pair(k - 1)
 
         @pl.when(k >= 2)
         def _():
-            j = k - 2
-            total = part[j, pl.ds(pl.multiple_of(lo * rows_lo + hi * rows_d, rows_d), rows_d), :]
-            for o in range(1, n_hi):
-                s2_copy(j, o).wait_recv()
-                total = total + recv2[j, o - 1]
-            fin[j] = total
-
-            @pl.when(j < normal)
-            def _():
-                for o in range(1, n_row):
-                    r_copy(j, o).start()
-                out_ref[:, out_cols(j)] = fin[j, pl.ds(pl.multiple_of(row * rows_r, rows_r), rows_r), :]
-
-            @pl.when(j >= normal)
-            def _():
-                for o in range(n_row):
-                    d_copy(j, o).start()
+            finish(k - 2)
 
         return c
 
-    lax.fori_loop(0, total_steps + 2, step, 0)
+    lax.fori_loop(0, normal, step, 0)
+
+    @pl.when(helps)
+    def _():
+        place_peers(1)
+        if gathered:
+            for p in range(n_swap, n_depth):
+                take(p)
+            plain_groups()
+        d_multiply(0)
+
+    pair(normal - 1)
+    finish(normal - 2)
+
+    @pl.when(helps)
+    def _():
+        d_multiply(1)
+        d_pair(0)
+
+    finish(normal - 1)
+
+    @pl.when(helps)
+    def _():
+        d_pair(1)
+        d_finish(0)
+        d_finish(1)
+        for p in range(n_swap, n_depth):
+            if not gathered:
+                take(p)
+            place_own(p)
+            place_peers(p)
+        d_multiply(2)
+        d_multiply(3)
+        d_pair(2)
+        d_pair(3)
+        d_finish(2)
+        d_finish(3)
 
     def drain(k, c):
         s1_copy(k).wait_send()
         for o in range(1, n_hi):
             s2_copy(k, o).wait_send()
-
-        @pl.when(k < normal)
-        def _():
-            for o in range(1, n_row):
-                r_copy(k, o).wait_send()
-                r_copy(k, o).wait_recv()
-
-        @pl.when(k >= normal)
-        def _():
+        for o in range(1, n_row):
+            r_copy(k, o).wait_send()
+            r_copy(k, o).wait_recv()
+        return c
+
+    lax.fori_loop(0, normal, drain, 0)
+
+    @pl.when(helps)
+    def _():
+        for n in range(2 * n_ch):
+            d1_copy(n).wait_send()
+            for o in range(1, n_hi):
+                d2_copy(n, o).wait_send()
             for o in range(n_row):
-                d_copy(k, o).wait_send()
-
-        return c
-
-    lax.fori_loop(0, total_steps, drain, 0)
+                d_copy(n, o).wait_send()
 
     near_sends("wait_send", 1)
 
@@ -432,9 +515,9 @@
             if not gathered:
                 for o in range(1, n_row):
                     f_copy(p, o).wait_send()
-        for h in range(n_ch):
+        for n in range(2 * n_ch):
             for o in range(n_row):
-                d_copy(h, o).wait_recv()
+                d_copy(n, o).wait_recv()
 
     if not gathered:
 
@@ -457,7 +540,8 @@
     j_count = j_local * n_row
     ab_rows = integrals.shape[0]
     n_ch = ab_rows // CHUNK
-    slots = (n_col + 1) * n_ch
+    slots = n_col * n_ch
+    late = 2 * n_ch
     rows_all = i_count * j_count
     rows_lo = rows_all // n_lo
     rows_d = rows_lo // n_hi
@@ -468,6 +552,7 @@
     tiny = j_local if gathered else n_row
     source = np.arange(side).reshape(i_out, j_local // tiny, tiny).transpose(2, 0, 1).reshape(-1)
     order = jnp.asarray(np.eye(side)[source], jnp.bfloat16)
+    assert i_out == n_depth
     t = jnp.transpose(amplitudes, (1, 2, 0))
     if gathered:
         t = lax.all_gather(t, "row", axis=1, tiled=True)
@@ -475,6 +560,7 @@
         t = jnp.transpose(t, (1, 0, 4, 2, 3, 5)).reshape(rows_all, kc)
         tg = pltpu.VMEM(t.shape, jnp.float32)
     else:
+        t = t.reshape(n_depth, i_out, j_local, kc)
         tg = pltpu.VMEM((n_row,) + t.shape, jnp.float32)
     dma = pltpu.SemaphoreType.DMA
     out = pl.pallas_call(
@@ -492,6 +578,10 @@
             pltpu.VMEM((slots, rows_lo, CHUNK), jnp.float32),
             pltpu.VMEM((slots, max(n_hi - 1, 1), rows_d, CHUNK), jnp.float32),
             pltpu.VMEM((slots, rows_d, CHUNK), jnp.float32),
+            pltpu.VMEM((late, rows_all // 2, CHUNK), jnp.float32),
+            pltpu.VMEM((late, rows_lo // 2, CHUNK), jnp.float32),
+            pltpu.VMEM((late, max(n_hi - 1, 1), rows_d // 2, CHUNK), jnp.float32),
+            pltpu.VMEM((late, rows_d // 2, CHUNK), jnp.float32),
             dma((2,)),
             dma((2, n_col, ab_rows // CHUNK)),
             dma((n_col, ab_rows // CHUNK)),
@@ -509,8 +599,12 @@
             dma((n_depth, max(n_row - 1, 1))),
             dma((n_depth, max(n_row - 1, 1))),
             dma((n_depth, max(n_row - 1, 1))),
-            dma((n_ch, n_row)),
-            dma((n_ch, n_row)),
+            dma((late,)),
+            dma((late,)),
+            dma((late, max(n_hi - 1, 1))),
+            dma((late, max(n_hi - 1, 1))),
+            dma((late, n_row)),
+            dma((late, n_row)),
         ],
         compiler_params=pltpu.CompilerParams(
             collective_id=0, has_side_effects=True, vmem_limit_bytes=60 * 2**20

time: 151 us -> 143 us (0.947)
  Pallas kernels: 148 us -> 139 us
    pallas_call x1, Pallas kernels: 148 us -> 139 us  [shards(): pl.pallas_call(functools.partial(kernel, sizes, gathered), out_shape=jax....]
where the time goes in v6:
time: 143 us; the launch traced here: 142 us
  Pallas kernels  139 us (97%)
  local copies, waits for them, and re-layouts  3.11 us (2%)
    pallas_call x1, Pallas kernels, shards(): pl.pallas_call(functools.partial(kernel, sizes, gathered), out_shape=jax....  139 us
    unnamed x1, local copies, waits for them, and re-layouts  3.11 us

profile of v6, /device:TPU:0, one launch (start us, length us, event | category | flops | bytes accessed | tf_op | source)
XLA Modules:
  0.0 142.4 jit_solution(14717460328349360390)
XLA Ops:
  0.0 139.3 %shard_map.37 = f32[128,4096]{1,0:T(8,128)} custom-call(f32[512,1024]{1,0:T(8,128)} %w_ref.1, f32[4,4,32,1024]{3,2,1,0:T(8,128)} %bitcast.5, bf16[128,128]{1,0:T(8,128)(2,1)} %constant.2.clone.order_ref), custom_call_target="tpu_custom_call" | custom-call | flops 12884901888 | bytes 6291456 | tf_op jit(solution)/shard_map/pallas_call | solution.py:566
  139.3 3.1 %copy.5 = f32[4,32,4096]{2,1,0:T(8,128)} copy(f32[4,32,4096]{2,1,0:T(8,128)} %bitcast.4) | data formatting | bytes 4194304

commit v7 on v6

--- a/solution.py
+++ b/solution.py
@@ -20,7 +20,7 @@
 
 
 def kernel(sizes, gathered, w_ref, t_ref, order_ref, out_ref, wg, tg, tg2, th, tl, part, recv1, recv2, fin,
-           part_d, recv1_d, recv2_d, fin_d,
+           part_d, recv1_d, recv2_d, fin_d, w_far,
            own_sem, w_send, w_recv, t_send, t_recv, s1_send, s1_recv, s2_send, s2_recv, r_send, r_recv,
            e_send, e_recv, f_send, f_recv, x_send, x_recv, d1_send, d1_recv, d2_send, d2_recv, d_send, d_recv):
     n_row, n_col, n_depth = sizes
@@ -177,8 +177,8 @@
             y = jnp.dot(order_ref[...], x_part, preferred_element_type=jnp.float32).astype(jnp.bfloat16)
             for n in range(n_row * n_depth):
                 r, d = n // n_depth, n % n_depth
-                base = (p // 2) * rows_all + (d % n_lo) * rows_lo + (d // n_lo) * rows_d + r * rows_r
-                at = base // 2 + (p % 2) * (per_r * n_row) + q * per_r
+                base = p * rows_all + (d % n_lo) * rows_lo + (d // n_lo) * rows_d + r * rows_r
+                at = base // n_depth + q * per_r
                 into[1, pl.ds(pl.multiple_of(at, per_r), per_r), :] = y[n * per_r : (n + 1) * per_r]
 
     def plain_groups():
@@ -199,6 +199,7 @@
 
     piece = rows_all // n_depth
     n_swap = n_depth // 2
+    n_g = 2 if gathered else n_depth
 
     def e_copy(p):
         rows = pl.ds(p * piece, piece)
@@ -317,7 +318,7 @@
 
     def d1_copy(n):
         return pltpu.make_async_remote_copy(
-            src_ref=part_d.at[n, pl.ds(pl.multiple_of((1 - lo) * (rows_lo // 2), rows_lo // 2), rows_lo // 2)],
+            src_ref=part_d.at[n, pl.ds(pl.multiple_of((1 - lo) * (rows_lo // n_g), rows_lo // n_g), rows_lo // n_g)],
             dst_ref=recv1_d.at[n],
             send_sem=d1_send.at[n],
             recv_sem=d1_recv.at[n],
@@ -326,9 +327,9 @@
         )
 
     def d2_copy(n, o):
-        start = lo * (rows_lo // 2) + hi_peer(o) * (rows_d // 2)
-        return pltpu.make_async_remote_copy(
-            src_ref=part_d.at[n, pl.ds(pl.multiple_of(start, rows_d // 2), rows_d // 2)],
+        start = lo * (rows_lo // n_g) + hi_peer(o) * (rows_d // n_g)
+        return pltpu.make_async_remote_copy(
+            src_ref=part_d.at[n, pl.ds(pl.multiple_of(start, rows_d // n_g), rows_d // n_g)],
             dst_ref=recv2_d.at[n, o - 1],
             send_sem=d2_send.at[n, o - 1],
             recv_sem=d2_recv.at[n, o - 1],
@@ -338,7 +339,7 @@
 
     def d_copy(n, o):
         g, h = n // n_ch, n % n_ch
-        half = rows_r // 2
+        half = rows_r // n_g
         return pltpu.make_async_remote_copy(
             src_ref=fin_d.at[n, pl.ds(pl.multiple_of(row_peer(o) * half, half), half)],
             dst_ref=out_ref.at[pl.ds(g * half, half), out_cols(far, h)],
@@ -348,9 +349,8 @@
             device_id_type=MESH,
         )
 
-    def multiply(b, h, which, first, tile):
-        w_t = wg[b, pl.ds(pl.multiple_of(h * CHUNK, CHUNK), CHUNK), :].T
-        wh, wl = halves(w_t)
+    def multiply(w_halves, which, first, tile):
+        wh, wl = w_halves
         w3 = jnp.concatenate([wh, wh, wl], axis=0)
         for start in first:
             at = pl.ds(start, tile)
@@ -359,20 +359,22 @@
             yield start, jnp.dot(a3, w3, preferred_element_type=jnp.float32)
 
     def d_multiply(n):
-        for _, y in multiply(far, n % n_ch, 1, (n // n_ch * (rows_all // 2),), rows_all // 2):
+        rows = rows_all // n_g
+        h = n % n_ch
+        for _, y in multiply((w_far[h, 0], w_far[h, 1]), 1, (n // n_ch * rows,), rows):
             part_d[n] = y
         d1_copy(n).start()
 
     def d_pair(n):
         d1_copy(n).wait_recv()
-        at = pl.ds(pl.multiple_of(lo * (rows_lo // 2), rows_lo // 2), rows_lo // 2)
+        at = pl.ds(pl.multiple_of(lo * (rows_lo // n_g), rows_lo // n_g), rows_lo // n_g)
         part_d[n, at, :] = part_d[n, at, :] + recv1_d[n]
         for o in range(1, n_hi):
             d2_copy(n, o).start()
 
     def d_finish(n):
-        start = lo * (rows_lo // 2) + hi * (rows_d // 2)
-        total = part_d[n, pl.ds(pl.multiple_of(start, rows_d // 2), rows_d // 2), :]
+        start = lo * (rows_lo // n_g) + hi * (rows_d // n_g)
+        total = part_d[n, pl.ds(pl.multiple_of(start, rows_d // n_g), rows_d // n_g), :]
         for o in range(1, n_hi):
             d2_copy(n, o).wait_recv()
             total = total + recv2_d[n, o - 1]
@@ -399,11 +401,11 @@
         out_ref[:, out_cols(*block_at(j)[:2])] = mine
 
     def step(k, c):
-        @pl.when(helps & (k == steps - 4))
+        @pl.when(helps & (k == 1))
         def _():
             take(0)
 
-        @pl.when(helps & (k == steps - 3))
+        @pl.when(helps & (k == 3))
         def _():
             take(1)
 
@@ -413,16 +415,16 @@
             place_own(1)
             place_peers(0)
 
-        @pl.when(k == normal - 3)
+        @pl.when(k == 3)
         def _():
             near_sends("wait_send", 0)
             near_sends("start", 1)
 
-        @pl.when(at_end & (k == normal - 3))
-        def _():
-            for p in range(n_swap):
-                e_copy(p).wait_send()
-            for p in range(n_swap, n_depth):
+        for p in range(n_swap, n_depth):
+
+            @pl.when(at_end & (k == 2 * (p - n_swap)))
+            def _():
+                e_copy(p - n_swap).wait_send()
                 e_copy(p).start()
                 if not gathered:
                     for o in range(1, n_row):
@@ -434,7 +436,13 @@
         def _():
             w_copy(wg, b, h, 0).wait_recv()
 
-        for start, y in multiply(b, h, 0, (0, rows_all // 2), rows_all // 2):
+        w_halves = halves(wg[b, pl.ds(pl.multiple_of(h * CHUNK, CHUNK), CHUNK), :].T)
+
+        @pl.when(helps & (k >= steps - n_ch))
+        def _():
+            w_far[h, 0], w_far[h, 1] = w_halves
+
+        for start, y in multiply(w_halves, 0, (0, rows_all // 2), rows_all // 2):
             part[k, pl.ds(start, rows_all // 2), :] = y
         s1_copy(k).start()
 
@@ -449,6 +457,10 @@
         return c
 
     lax.fori_loop(0, normal, step, 0)
+
+    def group(act, g):
+        for h in range(n_ch):
+            act(g * n_ch + h)
 
     @pl.when(helps)
     def _():
@@ -457,34 +469,33 @@
             for p in range(n_swap, n_depth):
                 take(p)
             plain_groups()
-        d_multiply(0)
+        group(d_multiply, 0)
 
     pair(normal - 1)
     finish(normal - 2)
 
     @pl.when(helps)
     def _():
-        d_multiply(1)
-        d_pair(0)
+        group(d_multiply, 1)
+        group(d_pair, 0)
 
     finish(normal - 1)
 
     @pl.when(helps)
     def _():
-        d_pair(1)
-        d_finish(0)
-        d_finish(1)
-        for p in range(n_swap, n_depth):
-            if not gathered:
-                take(p)
-            place_own(p)
-            place_peers(p)
-        d_multiply(2)
-        d_multiply(3)
-        d_pair(2)
-        d_pair(3)
-        d_finish(2)
-        d_finish(3)
+        group(d_pair, 1)
+        group(d_finish, 0)
+        group(d_finish, 1)
+        for g in range(2, n_g):
+            take(g)
+            place_own(g)
+            place_peers(g)
+            group(d_multiply, g)
+            if g > 2:
+                group(d_finish, g - 1)
+            group(d_pair, g)
+        if n_g > 2:
+            group(d_finish, n_g - 1)
 
     def drain(k, c):
         s1_copy(k).wait_send()
@@ -499,7 +510,7 @@
 
     @pl.when(helps)
     def _():
-        for n in range(2 * n_ch):
+        for n in range(n_g * n_ch):
             d1_copy(n).wait_send()
             for o in range(1, n_hi):
                 d2_copy(n, o).wait_send()
@@ -515,7 +526,7 @@
             if not gathered:
                 for o in range(1, n_row):
                     f_copy(p, o).wait_send()
-        for n in range(2 * n_ch):
+        for n in range(n_g * n_ch):
             for o in range(n_row):
                 d_copy(n, o).wait_recv()
 
@@ -541,7 +552,8 @@
     ab_rows = integrals.shape[0]
     n_ch = ab_rows // CHUNK
     slots = n_col * n_ch
-    late = 2 * n_ch
+    n_g = 2 if j_local % (16 * n_row) != 0 else n_depth
+    late = n_g * n_ch
     rows_all = i_count * j_count
     rows_lo = rows_all // n_lo
     rows_d = rows_lo // n_hi
@@ -578,10 +590,11 @@
             pltpu.VMEM((slots, rows_lo, CHUNK), jnp.float32),
             pltpu.VMEM((slots, max(n_hi - 1, 1), rows_d, CHUNK), jnp.float32),
             pltpu.VMEM((slots, rows_d, CHUNK), jnp.float32),
-            pltpu.VMEM((late, rows_all // 2, CHUNK), jnp.float32),
-            pltpu.VMEM((late, rows_lo // 2, CHUNK), jnp.float32),
-            pltpu.VMEM((late, max(n_hi - 1, 1), rows_d // 2, CHUNK), jnp.float32),
-            pltpu.VMEM((late, rows_d // 2, CHUNK), jnp.float32),
+            pltpu.VMEM((late, rows_all // n_g, CHUNK), jnp.float32),
+            pltpu.VMEM((late, rows_lo // n_g, CHUNK), jnp.float32),
+            pltpu.VMEM((late, max(n_hi - 1, 1), rows_d // n_g, CHUNK), jnp.float32),
+            pltpu.VMEM((late, rows_d // n_g, CHUNK), jnp.float32),
+            pltpu.VMEM((n_ch, 2, kc, CHUNK), jnp.bfloat16),
             dma((2,)),
             dma((2, n_col, ab_rows // CHUNK)),
             dma((n_col, ab_rows // CHUNK)),

time: 143 us -> 139 us (0.972)
  Pallas kernels: 139 us -> 136 us
    pallas_call x1, Pallas kernels: 139 us -> 136 us  [shards(): pl.pallas_call(functools.partial(kernel, sizes, gathered), out_shape=jax....]
where the time goes in v7:
time: 139 us
  Pallas kernels  136 us (98%)
  local copies, waits for them, and re-layouts  3.11 us (2%)
    pallas_call x1, Pallas kernels, shards(): pl.pallas_call(functools.partial(kernel, sizes, gathered), out_shape=jax....  136 us
    unnamed x1, local copies, waits for them, and re-layouts  3.11 us

profile of v7, /device:TPU:0, one launch (start us, length us, event | category | flops | bytes accessed | tf_op | source)
XLA Modules:
  0.0 139.0 jit_solution(16972139927084625042)
XLA Ops:
  0.0 135.8 %shard_map.37 = f32[128,4096]{1,0:T(8,128)} custom-call(f32[512,1024]{1,0:T(8,128)} %w_ref.1, f32[4,4,32,1024]{3,2,1,0:T(8,128)} %bitcast.5, bf16[128,128]{1,0:T(8,128)(2,1)} %constant.2.clone.order_ref), custom_call_target="tpu_custom_call" | custom-call | flops 12884901888 | bytes 6291456 | tf_op jit(solution)/shard_map/pallas_call | solution.py:578
  135.8 3.1 %copy.5 = f32[4,32,4096]{2,1,0:T(8,128)} copy(f32[4,32,4096]{2,1,0:T(8,128)} %bitcast.4) | data formatting | bytes 4194304

commit v8 on v7

--- a/solution.py
+++ b/solution.py
@@ -132,19 +132,20 @@
 
     own_sends("start", 0)
 
-    def t_copy(o):
-        return pltpu.make_async_remote_copy(
-            src_ref=t_ref,
-            dst_ref=tg.at[row],
-            send_sem=t_send.at[o - 1],
-            recv_sem=t_recv.at[o - 1],
+    def t_copy(o, d):
+        return pltpu.make_async_remote_copy(
+            src_ref=t_ref.at[d],
+            dst_ref=tg.at[row, d],
+            send_sem=t_send.at[o - 1, d],
+            recv_sem=t_recv.at[o - 1, d],
             device_id={"row": row_peer(o)},
             device_id_type=MESH,
         )
 
     if not gathered:
-        for o in range(1, n_row):
-            t_copy(o).start()
+        for d in range(n_depth):
+            for o in range(1, n_row):
+                t_copy(o, d).start()
         t_own = pltpu.make_async_copy(t_ref, tg.at[row], own_sem.at[1])
     else:
         t_own = pltpu.make_async_copy(t_ref, tg, own_sem.at[1])
@@ -152,7 +153,7 @@
     w_own = pltpu.make_async_copy(w_ref, wg.at[col], own_sem.at[0])
     w_own.start()
 
-    def place(src, q):
+    def place(src, q, first, last):
         i_out, j_local, kc = t_ref.shape[1:]
         per_r = j_local // n_row
         order = order_ref[...]
@@ -167,7 +168,7 @@
                     into[0, pl.ds(pl.multiple_of(at, per_r), per_r), :] = y[n * per_r : (n + 1) * per_r]
             return c
 
-        lax.fori_loop(0, n_depth, body, 0)
+        lax.fori_loop(first, last, body, 0)
 
     def place_piece(q, p):
         i_out, j_local, kc = t_ref.shape[1:]
@@ -251,7 +252,7 @@
 
     t_own.wait()
     if not gathered:
-        place(tg, row)
+        place(tg, row, 0, n_depth)
     else:
         plain()
 
@@ -268,9 +269,10 @@
 
     near_arrive(1)
     if not gathered:
-        for o in range(1, n_row):
-            t_copy(o).wait_recv()
-            place(tg, (row + n_row - o) % n_row)
+        for d in range(n_depth):
+            for o in range(1, n_row):
+                t_copy(o, d).wait_recv()
+                place(tg, (row + n_row - o) % n_row, d, d + 1)
     w_own.wait()
 
     near = jnp.minimum(col, n_col - 1 - col)
@@ -539,8 +541,9 @@
                     x_copy(p, o).wait_send()
 
     if not gathered:
-        for o in range(1, n_row):
-            t_copy(o).wait_send()
+        for d in range(n_depth):
+            for o in range(1, n_row):
+                t_copy(o, d).wait_send()
 
 
 def shards(sizes, integrals, amplitudes):
@@ -598,8 +601,8 @@
             dma((2,)),
             dma((2, n_col, ab_rows // CHUNK)),
             dma((n_col, ab_rows // CHUNK)),
-            dma((max(n_row - 1, 1),)),
-            dma((max(n_row - 1, 1),)),
+            dma((max(n_row - 1, 1), n_depth)),
+            dma((max(n_row - 1, 1), n_depth)),
             dma((slots,)),
             dma((slots,)),
             dma((slots, max(n_hi - 1, 1))),

time: 139 us -> 139 us (level)
  no operation moved by 1% of the time
where the time goes in v8:
time: 139 us
  Pallas kernels  136 us (98%)
  local copies, waits for them, and re-layouts  3.11 us (2%)
    pallas_call x1, Pallas kernels, shards(): pl.pallas_call(functools.partial(kernel, sizes, gathered), out_shape=jax....  136 us
    unnamed x1, local copies, waits for them, and re-layouts  3.11 us

profile of v8, /device:TPU:0, one launch (start us, length us, event | category | flops | bytes accessed | tf_op | source)
XLA Modules:
  0.0 139.0 jit_solution(12345386921495934927)
XLA Ops:
  0.0 135.9 %shard_map.37 = f32[128,4096]{1,0:T(8,128)} custom-call(f32[512,1024]{1,0:T(8,128)} %w_ref.1, f32[4,4,32,1024]{3,2,1,0:T(8,128)} %bitcast.5, bf16[128,128]{1,0:T(8,128)(2,1)} %constant.2.clone.order_ref), custom_call_target="tpu_custom_call" | custom-call | flops 12884901888 | bytes 6291456 | tf_op jit(solution)/shard_map/pallas_call | solution.py:581
  135.9 3.1 %copy.5 = f32[4,32,4096]{2,1,0:T(8,128)} copy(f32[4,32,4096]{2,1,0:T(8,128)} %bitcast.4) | data formatting | bytes 4194304

commit v9 on v7

--- a/solution.py
+++ b/solution.py
@@ -198,7 +198,7 @@
         lax.fori_loop(0, rows_all // 64, body, 0)
 
     piece = rows_all // n_depth
-    n_swap = n_depth // 2
+    n_swap = n_depth - 1
     n_g = 2 if gathered else n_depth
 
     def e_copy(p):
@@ -263,8 +263,8 @@
 
     @pl.when(at_end)
     def _():
-        e_copy(0).start()
-        e_copy(1).start()
+        for p in range(n_swap):
+            e_copy(p).start()
 
     near_arrive(1)
     if not gathered:
@@ -409,6 +409,10 @@
         def _():
             take(1)
 
+        @pl.when(helps & (k == 4))
+        def _():
+            take(2)
+
         @pl.when(helps & (k == steps - 1))
         def _():
             place_own(0)
@@ -487,7 +491,8 @@
         group(d_finish, 0)
         group(d_finish, 1)
         for g in range(2, n_g):
-            take(g)
+            if g >= n_swap:
+                take(g)
             place_own(g)
             place_peers(g)
             group(d_multiply, g)
@@ -521,6 +526,8 @@
 
     @pl.when(at_end)
     def _():
+        for p in range(n_depth - n_swap, n_swap):
+            e_copy(p).wait_send()
         for p in range(n_swap, n_depth):
             e_copy(p).wait_send()
             if not gathered:

time: 139 us -> 145 us (1.043)
  Pallas kernels: 136 us -> 141 us
    pallas_call x1, Pallas kernels: 136 us -> 141 us  [shards(): pl.pallas_call(functools.partial(kernel, sizes, gathered), out_shape=jax....]
where the time goes in v9:
time: 145 us
  Pallas kernels  141 us (97%)
  local copies, waits for them, and re-layouts  3.11 us (2%)
    pallas_call x1, Pallas kernels, shards(): pl.pallas_call(functools.partial(kernel, sizes, gathered), out_shape=jax....  141 us
    unnamed x1, local copies, waits for them, and re-layouts  3.11 us

profile of v9, /device:TPU:0, one launch (start us, length us, event | category | flops | bytes accessed | tf_op | source)
XLA Modules:
  0.0 144.6 jit_solution(16189241046374967627)
XLA Ops:
  0.0 141.5 %shard_map.37 = f32[128,4096]{1,0:T(8,128)} custom-call(f32[512,1024]{1,0:T(8,128)} %w_ref.1, f32[4,4,32,1024]{3,2,1,0:T(8,128)} %bitcast.5, bf16[128,128]{1,0:T(8,128)(2,1)} %constant.2.clone.order_ref), custom_call_target="tpu_custom_call" | custom-call | flops 12884901888 | bytes 6291456 | tf_op jit(solution)/shard_map/pallas_call | solution.py:585
  141.5 3.1 %copy.5 = f32[4,32,4096]{2,1,0:T(8,128)} copy(f32[4,32,4096]{2,1,0:T(8,128)} %bitcast.4) | data formatting | bytes 4194304
